TPU v7x, 32 devices: a whole 2x2x4 slice. The times are simulated.
32 devices in a mesh: grp: 2 (over x), tract: 16 (over z, y, core).
Axes of the slice: x: 2, y: 2, z: 4, core: 2. Of those that a mesh axis runs over, the one named last changes fastest.
Arguments:
- table: float32 [384, 23, 7, 7, 128], P(('grp', 'tract')), parts along dimension 0, may hold values from 0.25 to 4
- age_sex: float32 [384, 46], P(('grp', 'tract')), parts along dimension 0, may hold values from 1960 to 15680
- race_hisp: float32 [384, 14], P(('grp', 'tract')), parts along dimension 0, may hold values from 6440 to 51520
- size_tenure: float32 [384, 14], P(('grp', 'tract')), parts along dimension 0, may hold values from 6440 to 51520
- tenure_income: float32 [384, 32], P(('grp', 'tract')), parts along dimension 0, may hold values from 2817.5 to 22540
- puma_age: float32 [48, 1472], P('grp'), parts along dimension 0, may hold values from 3920 to 31360
- puma_race: float32 [48, 3136], P('grp'), parts along dimension 0, may hold values from 1840 to 14720
- tract_puma: int32 [384], P(('grp', 'tract')), parts along dimension 0, may hold values from 0 to 23, as said below
Outputs:
- raked: float32 [384, 23, 7, 7, 128], P(('grp', 'tract')), parts along dimension 0
There are 2 independent parts, one for each index of `grp`. A program takes and returns all parts, laid end to end along the dimension named above; each array names one. Nothing has to cross between parts.
Inputs may be any that keep to these rules, and one draw needn't show every extreme that they name: `tract_puma`: each PUMA holds exactly 8 tracts, which may lie anywhere in the tract order.
All inputs are finite; a program needn't handle non-finite values.
Results may differ from a plain program's by a relative error of at most 0.000092.
Values sent between devices are 32-bit elements; how exact they have to be, the bound alone decides.
No kernel may reach another device: no remote copies, remote signals or barrier semaphores. Data moves between devices by JAX's collectives and lax.ppermute only.
A program may use at most 64 MiB of HBM per device.

v0:
```python
import functools

import jax
import jax.numpy as jnp
from jax import lax
from jax.experimental import pallas as pl
from jax.experimental.pallas import tpu as pltpu
from jax.sharding import PartitionSpec as P

LANES = 128
GROUP = 6
FIRST = 6
F32 = jnp.float32


def round_up(value, step):
    return -(-value // step) * step


def lane_ids(rows):
    return lax.broadcasted_iota(jnp.int32, (rows, LANES), 1)


def masked_lane_sum(value, mask):
    return jnp.sum(jnp.where(mask, value, 0.0), axis=-1, keepdims=True)


def column_of(row, rows, step, offset):
    width = row.shape[-1]
    lane = lax.broadcasted_iota(jnp.int32, (rows, width), 1)
    sub = lax.broadcasted_iota(jnp.int32, (rows, width), 0)
    return jnp.sum(jnp.where(lane == step * sub + offset, row, 0.0), axis=-1, keepdims=True)


def half_of(index):
    total = index
    for k in range(1, 16):
        total = total + lax.shift_right_logical(index, k)
    return lax.rem(total, 2)


def factor_rows(target_ref, own_refs, other_refs, rows_ref):
    pumas, columns = target_ref.shape
    half = half_of(lax.axis_index("tract"))
    half_rows = sum(ref.shape[0] for ref in own_refs)
    for refs, which in ((own_refs, half), (other_refs, 1 - half)):
        start = which * half_rows
        for ref in refs:
            rows_ref[pl.ds(pl.multiple_of(start, 8), ref.shape[0]), :] = ref[...]
            start = start + ref.shape[0]
    for first in range(0, columns, LANES):
        width = min(columns - first, LANES)
        at = slice(first // LANES * pumas, (first // LANES + 1) * pumas)
        rows_ref[at, 0:width] = target_ref[:, first : first + width] / rows_ref[at, 0:width]


def load_puma_numbers(ids_ref, scalar_ref):
    ids = ids_ref[...]
    for t in range(scalar_ref.shape[0]):
        scalar_ref[t] = ids[t]


def put_halves(rows_ref, keep_refs, send_refs):
    half = half_of(lax.axis_index("tract"))
    half_rows = sum(ref.shape[0] for ref in keep_refs)
    for refs, which in ((keep_refs, half), (send_refs, 1 - half)):
        start = which * half_rows
        for ref in refs:
            ref[...] = rows_ref[pl.ds(pl.multiple_of(start, 8), ref.shape[0]), :]
            start = start + ref.shape[0]


def merge(first, second, step):
    low = lax.rem(lax.broadcasted_iota(jnp.int32, (8, 1), 0) // step, 2) == 0
    if step == 4:
        return jnp.where(low, first, second) + pltpu.roll(jnp.where(low, second, first), 4, 0)
    return jnp.where(low, first + pltpu.roll(first, 8 - step, 0), second + pltpu.roll(second, step, 0))


def each(start, stop, body, width=3):
    def turn(i, carry):
        for k in range(width):
            body(start + width * i + k)
        return carry

    turns = (stop - start) // width
    lax.fori_loop(0, turns, turn, 0)
    for t in range(start + width * turns, stop):
        body(t)


def age_sums(cells_ref, factor, cross_ref, base, count):
    ages = factor.shape[0]

    def tile(k):
        total = None
        for at in range(0, ages, 8):
            stop = min(at + 8, ages)
            part = cells_ref[k, at:stop] * factor[at:stop]
            if stop < at + 8:
                part = jnp.concatenate([part, jnp.zeros((at + 8 - stop, LANES), F32)], axis=0)
            total = part if total is None else total + part
        return total

    for start in range(0, count, 8):
        tiles = [tile(k) for k in range(start, min(start + 8, count))]
        if len(tiles) < 8:
            for k, x in enumerate(tiles):
                cross_ref[pl.ds(base + start + k, 1), :] = jnp.sum(x, axis=0, keepdims=True)
            continue
        tiles = [merge(tiles[k], tiles[k + 4], 4) for k in range(4)]
        tiles = [merge(tiles[k], tiles[k + 2], 2) for k in range(2)]
        cross_ref[pl.ds(pl.multiple_of(base + start, 8), 8), :] = merge(tiles[0], tiles[1], 1)


def pair_sum(term, count):
    first, second = term(0), term(1)
    for k in range(2, count, 2):
        first = first + term(k)
        if k + 1 < count:
            second = second + term(k + 1)
    return first + second


def rake_kernel(
    ids_hbm, table_hbm, age_sex_hbm, race_hisp_hbm, size_tenure_hbm, tenure_income_hbm,
    keep_ref, send_ref, age_factor_ref, cross_factor_ref, cells_ref,
    sum_ref, cross_ref, rows_ref, age_target_ref, race_target_ref, size_target_ref,
    ids_ref, age_sex_ref, race_hisp_ref, size_tenure_ref, tenure_income_ref,
    sems, small_sems,
    *, races, sizes, pumas,
):
    tracts, cross, ages, _ = table_hbm.shape
    cross_rows = round_up(cross + 1, 8)
    pairs = (ages + 1) // 2
    small = [
        pltpu.make_async_copy(source, target, small_sems.at[i])
        for i, (source, target) in enumerate((
            (ids_hbm, ids_ref),
            (age_sex_hbm, age_sex_ref),
            (race_hisp_hbm, race_hisp_ref),
            (size_tenure_hbm, size_tenure_ref),
            (tenure_income_hbm, tenure_income_ref),
        ))
    ]

    def table_copy(t):
        return pltpu.make_async_copy(table_hbm.at[t], cells_ref.at[t, 0:cross], sems.at[t])

    for copy in small:
        copy.start()
    for t in range(min(FIRST, tracts)):
        table_copy(t).start()
    lane = lane_ids(1)
    sex0 = lane < 64
    hisp0 = (lane // 32) % 2 == 0
    ten0 = (lane // 16) % 2 == 0

    rows_ref[...] = jnp.zeros(rows_ref.shape, F32)
    for copy in small:
        copy.wait()
    for source_ref, target_ref, rows, mask in (
        (age_sex_ref, age_target_ref, ages, sex0),
        (race_hisp_ref, race_target_ref, races, hisp0),
        (size_tenure_ref, size_target_ref, sizes, ten0),
    ):
        for t in range(tracts):
            row = source_ref[t : t + 1, :]
            target_ref[t, 0:rows] = jnp.where(
                mask, column_of(row, rows, 2, 0), column_of(row, rows, 2, 1)
            )

    for t in range(FIRST, tracts):
        table_copy(t).start()

    def group_sums(values, mask):
        first = [masked_lane_sum(x, mask) for x in values]
        second = [masked_lane_sum(x, ~mask) for x in values]
        return [jnp.where(mask, x, y) for x, y in zip(first, second)]

    def arrive(t):
        table_copy(t).wait()
        sum_ref[t, 0:ages] = pair_sum(lambda rs: cells_ref[t, rs], cross)

    def add_ages(t):
        age_sums(cells_ref.at[t], age_factor_ref[t, 0:ages], cross_ref, t * cross_rows, cross)

    def add_scaled(t):
        base = t * cross_rows
        total = pair_sum(
            lambda rs: cells_ref[t, rs] * cross_factor_ref[pl.ds(base + rs, 1), :], cross
        )
        sum_ref[t, 0:ages] = total * age_factor_ref[t, 0:ages]
        sum_ref[t, ages : 2 * pairs] = jnp.zeros((2 * pairs - ages, LANES), F32)

    def small_steps(group):
        bases = [t * cross_rows for t in group]
        by_race = [
            sum(cross_ref[pl.ds(base + s, races, stride=sizes), :] for s in range(sizes))
            for base in bases
        ]
        race_factor = [
            race_target_ref[t, 0:races] / margin for t, margin in zip(group, group_sums(by_race, hisp0))
        ]
        by_size = [
            sum(
                cross_ref[pl.ds(base + r * sizes, sizes), :] * factor[r : r + 1]
                for r in range(races)
            )
            for base, factor in zip(bases, race_factor)
        ]
        size_factor = [
            size_target_ref[t, 0:sizes] / margin for t, margin in zip(group, group_sums(by_size, ten0))
        ]
        by_income = [jnp.sum(x * y, axis=0, keepdims=True) for x, y in zip(by_size, size_factor)]
        by_income = [x + pltpu.roll(x, 64, 1) for x in by_income]
        by_income = [x + pltpu.roll(x, 32, 1) for x in by_income]
        for i, t in enumerate(group):
            target = jnp.concatenate([tenure_income_ref[t : t + 1, :]] * 4, axis=1)
            age_factor_ref[t, 0:ages] = age_factor_ref[t, 0:ages] * (target / by_income[i])
            for r in range(races):
                cross_factor_ref[pl.ds(bases[i] + r * sizes, sizes), :] = (
                    size_factor[i] * race_factor[i][r : r + 1]
                )
            cross_factor_ref[pl.ds(bases[i] + cross, cross_rows - cross), :] = jnp.zeros(
                (cross_rows - cross, LANES), F32
            )

    def pack(group):
        even = [sum_ref[t, pl.ds(0, pairs, stride=2)] for t in group]
        odd = [sum_ref[t, pl.ds(1, pairs, stride=2)] for t in group]
        even = [x + pltpu.roll(x, 96, 1) for x in even]
        odd = [x + pltpu.roll(x, 96, 1) for x in odd]
        packed = [
            jnp.where(
                lane < 32,
                x,
                jnp.where(
                    lane < 64,
                    pltpu.roll(x, 96, 1),
                    jnp.where(lane < 96, pltpu.roll(y, 64, 1), pltpu.roll(y, 32, 1)),
                ),
            )
            for x, y in zip(even, odd)
        ]
        for t, x in zip(group, packed):
            at = pl.ds(ids_ref[t], pairs, stride=pumas)
            rows_ref[at, :] = rows_ref[at, :] + x

    def work(group):
        margin = group_sums([sum_ref[t, 0:ages] for t in group], sex0)
        for t, x in zip(group, margin):
            age_factor_ref[t, 0:ages] = age_target_ref[t, 0:ages] / x
        each(group.start, group.stop, add_ages)
        small_steps(group)
        each(group.start, group.stop, add_scaled)
        pack(group)

    before = None
    for start in range(0, tracts, GROUP):
        if before is not None:
            work(before)
        before = range(start, min(start + GROUP, tracts))
        each(before.start, before.stop, arrive, 1)
    work(before)
    put_halves(rows_ref, [keep_ref], [send_ref])


def race_half(cells_ref, factor_ref, cross_factor_ref, chunk_refs, cross_ref, rows_ref, scalar_ref, half, pumas, ages, cross):
    tracts = cells_ref.shape[0]
    cross_rows = round_up(cross + 1, 8)
    pairs = sum(ref.shape[0] for ref in chunk_refs) // pumas
    count = 2 * pairs
    stride = round_up(count, 8)
    rows_ref[...] = jnp.zeros(rows_ref.shape, F32)
    lane = lane_ids(1)

    def add_ages(t):
        factor = factor_ref[t, 0:ages]
        cells = cells_ref.at[t, pl.ds(half * count, count)]
        age_sums(cells, factor, cross_ref, t * stride, count)

    each(0, tracts, add_ages)
    every = range(tracts)
    halves = []
    for first in range(2):
        margin = [
            cross_ref[pl.ds(t * stride + first, pairs, stride=2), :]
            * cross_factor_ref[pl.ds(t * cross_rows + half * count + first, pairs, stride=2), :]
            for t in every
        ]
        halves.append([x + pltpu.roll(x, 64, 1) for x in margin])
    for t in every:
        at = pl.ds(scalar_ref[t], pairs, stride=pumas)
        rows_ref[at, :] = rows_ref[at, :] + jnp.where(lane < 64, halves[0][t], halves[1][t])
    start = 0
    for ref in chunk_refs:
        ref[...] = rows_ref[start : start + ref.shape[0], :]
        start += ref.shape[0]


def race_send_kernel(
    ids_ref, cells_ref, age_factor_ref, cross_factor_ref, target_ref,
    own_ref, other_ref, *refs, cross
):
    *chunk_refs, scaled_factor_ref, cross_ref, age_rows_ref, rows_ref, scalar_ref = refs
    ages = 2 * (target_ref.shape[1] // LANES) + target_ref.shape[1] % LANES // 64
    pairs = (ages + 1) // 2
    pumas = target_ref.shape[0]
    every = range(cells_ref.shape[0])
    load_puma_numbers(ids_ref, scalar_ref)
    factor_rows(target_ref, [own_ref], [other_ref], age_rows_ref)
    lane = lane_ids(1)
    packed = [age_rows_ref[pl.ds(scalar_ref[t], pairs, stride=pumas), :] for t in every]
    quarter = [pltpu.roll(x, 32, 1) for x in packed]
    half = [pltpu.roll(x, 64, 1) for x in packed]
    back = [pltpu.roll(x, 96, 1) for x in packed]
    for t in every:
        even = jnp.where(lane < 32, packed[t], jnp.where(lane < 96, quarter[t], half[t]))
        odd = jnp.where(lane < 32, half[t], jnp.where(lane < 96, back[t], packed[t]))
        for first, factor in enumerate((even, odd)):
            at = pl.ds(first, pairs, stride=2)
            scaled_factor_ref[t, at] = factor * age_factor_ref[t, at]
    race_half(
        cells_ref, scaled_factor_ref, cross_factor_ref, chunk_refs, cross_ref, rows_ref, scalar_ref,
        1 - half_of(lax.axis_index("tract")), pumas, ages, cross,
    )


def race_keep_kernel(ids_ref, cells_ref, factor_ref, cross_factor_ref, *refs, ages, pumas, cross):
    *chunk_refs, cross_ref, rows_ref, scalar_ref = refs
    load_puma_numbers(ids_ref, scalar_ref)
    race_half(
        cells_ref, factor_ref, cross_factor_ref, chunk_refs, cross_ref, rows_ref, scalar_ref,
        half_of(lax.axis_index("tract")), pumas, ages, cross,
    )


def final_kernel(
    ids_ref, cells_ref, scaled_factor_ref, cross_factor_ref, target_ref, *refs
):
    *chunk_refs, out_ref, result_ref, cross_ref, rows_ref, scalar_ref, sems = refs
    chunks = len(chunk_refs) // 2
    tracts, cross, ages, _ = out_ref.shape
    cross_rows = round_up(cross + 1, 8)
    cross_pairs = (cross + 1) // 2
    pumas = target_ref.shape[0]
    load_puma_numbers(ids_ref, scalar_ref)
    factor_rows(target_ref, chunk_refs[:chunks], chunk_refs[chunks:], rows_ref)
    lane = lane_ids(1)

    def unpack(t):
        base = t * cross_rows
        packed = rows_ref[pl.ds(scalar_ref[t], cross_pairs, stride=pumas), :]
        half = pltpu.roll(packed, 64, 1)
        for first, factor in enumerate(
            (jnp.where(lane < 64, packed, half), jnp.where(lane < 64, half, packed))
        ):
            at = pl.ds(base + first, cross_pairs, stride=2)
            cross_ref[at, :] = factor * cross_factor_ref[at, :]

    def scale(t):
        factor = scaled_factor_ref[t, 0:ages]
        base = t * cross_rows
        for rs in range(cross):
            result_ref[t, rs] = cells_ref[t, rs] * factor * cross_ref[pl.ds(base + rs, 1), :]

    def send(t):
        pltpu.make_async_copy(result_ref.at[t], out_ref.at[t], sems.at[t]).start()

    def step(t, carry):
        scale(t)
        unpack(t + 1)
        send(t)
        return carry

    unpack(0)
    lax.fori_loop(0, tracts - 1, step, 0)
    scale(tracts - 1)
    send(tracts - 1)
    for t in range(tracts):
        pltpu.make_async_copy(result_ref.at[t], out_ref.at[t], sems.at[t]).wait()


def call(kernel, out_shapes, in_spaces, out_spaces, scratch):
    def spec(space):
        return pl.BlockSpec(memory_space=space)

    run = pl.pallas_call(
        kernel,
        out_shape=[
            space(shape, F32) for shape, space in zip(out_shapes, out_spaces, strict=True)
        ],
        in_specs=[spec(space) for space in in_spaces],
        out_specs=[spec(space) for space in out_spaces],
        scratch_shapes=scratch,
        compiler_params=pltpu.CompilerParams(vmem_limit_bytes=40 << 20),
    )

    def placed(*args):
        return run(*map(pltpu.with_memory_space_constraint, args, in_spaces))

    return placed


def per_device(
    devices,
    table, age_sex, race_hisp, size_tenure, tenure_income, puma_age, puma_race, tract_puma,
):
    tracts, ages, races, sizes, inner = table.shape
    pumas = puma_age.shape[0]
    cross = races * sizes
    age_pairs, cross_pairs = (ages + 1) // 2, (cross + 1) // 2
    age_rows = 2 * round_up(age_pairs, 8)
    cross_rows = tracts * round_up(cross + 1, 8) + 2 * round_up(cross_pairs, 8)
    age_sum_rows, cross_sum_rows = (round_up(x, 8) * pumas for x in (age_pairs, cross_pairs))
    vmem, hbm = pltpu.VMEM, pltpu.HBM

    cells = table.transpose(0, 2, 3, 1, 4).reshape(tracts, cross, ages, inner)
    cells_scratch = pltpu.VMEM((tracts, cross, ages, inner), F32)
    cross_scratch = pltpu.VMEM((cross_rows, LANES), F32)
    copy_sems = pltpu.SemaphoreType.DMA((tracts,))
    numbers_scratch = pltpu.SMEM((tracts,), jnp.int32)

    bits = [1 << k for k in range(1, devices.bit_length() - 1)]
    orders = (bits, bits[1:] + bits[:1])

    def swap(x, partner):
        return lax.ppermute(x, "tract", [(i, partner(i)) for i in range(devices)])

    def totals(keep, send):
        keep = [x + swap(y, lambda i: i ^ 1) for x, y in zip(keep, send)]
        for step in range(len(bits)):
            keep = [x + swap(x, lambda i: i ^ orders[i.bit_count() % 2][step] ^ 1) for x in keep]
        return *keep, *[swap(x, lambda i: i ^ 1) for x in keep]

    age_half, cross_half = -(-age_pairs // 2), -(-cross_pairs // 2)
    cross_chunks = [cross_half - cross_half // 2, cross_half // 2]
    age_shape, cross_shape = (tracts, age_rows, LANES), (cross_rows, LANES)
    small = [age_sex, race_hisp, size_tenure, tenure_income]
    keep, send, age_factor, cross_factor, cells = call(
        functools.partial(rake_kernel, races=races, sizes=sizes, pumas=pumas),
        [(age_half * pumas, LANES)] * 2
        + [age_shape, cross_shape, (tracts, 4 * cross_half, ages, inner)],
        [hbm] * 6,
        [vmem] * 5,
        [
            pltpu.VMEM(age_shape, F32),
            cross_scratch,
            pltpu.VMEM((age_sum_rows, LANES), F32),
            pltpu.VMEM(age_shape, F32),
            pltpu.VMEM((tracts, round_up(races, 8), LANES), F32),
            pltpu.VMEM((tracts, round_up(sizes, 8), LANES), F32),
            numbers_scratch,
        ]
        + [pltpu.VMEM(x.shape, F32) for x in small]
        + [copy_sems, pltpu.SemaphoreType.DMA((1 + len(small),))],
    )(tract_puma, cells, *small)

    half_scratch = [
        pltpu.VMEM((tracts * round_up(2 * cross_half, 8) + 16, LANES), F32),
        pltpu.VMEM((round_up(cross_half, 8) * pumas, LANES), F32),
    ]
    chunk_shapes = [(rows * pumas, LANES) for rows in cross_chunks]
    *send, scaled_factor = call(
        functools.partial(race_send_kernel, cross=cross),
        chunk_shapes + [age_shape],
        [vmem] * 7,
        [vmem] * (len(cross_chunks) + 1),
        [half_scratch[0], pltpu.VMEM((age_sum_rows, LANES), F32), half_scratch[1], numbers_scratch],
    )(tract_puma, cells, age_factor, cross_factor, puma_age, *totals([keep], [send]))
    keep = call(
        functools.partial(race_keep_kernel, ages=ages, pumas=pumas, cross=cross),
        chunk_shapes,
        [vmem] * 4,
        [vmem] * len(cross_chunks),
        half_scratch + [numbers_scratch],
    )(tract_puma, cells, scaled_factor, cross_factor)

    out, = call(
        final_kernel,
        [(tracts, cross, ages, inner)],
        [vmem] * (5 + 2 * len(cross_chunks)),
        [hbm],
        [
            cells_scratch,
            cross_scratch,
            pltpu.VMEM((cross_sum_rows, LANES), F32),
            numbers_scratch,
            copy_sems,
        ],
    )(tract_puma, cells, scaled_factor, cross_factor, puma_race, *totals(keep, send))
    return out.reshape(tracts, races, sizes, ages, inner).transpose(0, 3, 1, 2, 4)


def solution(mesh):
    in_specs = (
        P(("grp", "tract"), None, None, None, None),
        P(("grp", "tract"), None),
        P(("grp", "tract"), None),
        P(("grp", "tract"), None),
        P(("grp", "tract"), None),
        P("grp", None),
        P("grp", None),
        P(("grp", "tract")),
    )
    out_specs = P(("grp", "tract"), None, None, None, None)
    return jax.shard_map(
        functools.partial(per_device, mesh.shape["tract"]),
        mesh=mesh, in_specs=in_specs, out_specs=out_specs, check_vma=False,
    )
```

profile of v0, /device:TPU:13, one launch (start us, length us, event | category | flops | bytes accessed | tf_op | source)
XLA Modules:
  0.0 45.4 jit_solution(5218843595648113140)
XLA Ops:
  0.0 0.0 copy-start.2
  0.0 0.0 copy-start.1
  0.0 5.4 %shard_map.82 = (f32[144,128]{1,0:T(8,128)S(1)}, f32[144,128]{1,0:T(8,128)S(1)}, f32[12,32,128]{2,1,0:T(8,128)S(1)}, f32[736,128]{1,0:T(8,128)S(1)}, f32[12,52,23,128]{3,2,1,0:T(8,128)S(1)}) custom-call(s32[12]{0:T(128)} %ids_ref.5, f32[12,49,23,128]{3,2,1,0:T(8,128)} %bitcast.6, f32[12,46]{1,0:T(8,128)} %age_sex_hbm.1, f32[12,14]{1,0:T(8,128)} %race_hisp_hbm.1, ...), custom_call_target="tpu_custom_call" | custom-call | tf_op jit(solution)/shard_map/pallas_call | solution.py:401
  5.4 0.7 %collective-permute-start = (f32[144,128]{1,0:T(8,128)S(1)}, f32[144,128]{1,0:T(8,128)S(1)}, u32[]{:S(2)}, u32[]{:S(2)}) collective-permute-start(f32[144,128]{1,0:T(8,128)S(1)} %get-tuple-element.19), channel_id=1, source_target_pairs={{0,1},{1,0},{2,3},{3,2},{4,5},{5,4},{6,7},{7,6},{8,9},{9,8},{10,11... | collective-permute-start | bytes 221192 | tf_op jit(solution)/shard_map/ppermute | solution.py:429
  6.1 0.9 %collective-permute-done = f32[144,128]{1,0:T(8,128)S(1)} collective-permute-done((f32[144,128]{1,0:T(8,128)S(1)}, f32[144,128]{1,0:T(8,128)S(1)}, u32[]{:S(2)}, u32[]{:S(2)}) %collective-permute-start) | collective-permute-done | bytes 73760 | tf_op jit(solution)/shard_map/ppermute | solution.py:429
  7.1 0.5 %collective-permute-start.1 = (f32[144,128]{1,0:T(8,128)S(1)}, f32[144,128]{1,0:T(8,128)S(1)}, u32[]{:S(2)}, u32[]{:S(2)}) collective-permute-start(f32[144,128]{1,0:T(8,128)S(1)} %add.36), channel_id=1, source_target_pairs={{0,3},{1,4},{2,7},{3,0},{4,1},{5,6},{6,5},{7,2},{8,13},{9,10},{10,... | collective-permute-start | bytes 221192 | tf_op jit(solution)/shard_map/ppermute | solution.py:429
  7.5 3.4 %collective-permute-done.1 = f32[144,128]{1,0:T(8,128)S(1)} collective-permute-done((f32[144,128]{1,0:T(8,128)S(1)}, f32[144,128]{1,0:T(8,128)S(1)}, u32[]{:S(2)}, u32[]{:S(2)}) %collective-permute-start.1) | collective-permute-done | bytes 73760 | tf_op jit(solution)/shard_map/ppermute | solution.py:429
  10.9 2.6 %collective-permute-start.2 = (f32[144,128]{1,0:T(8,128)S(1)}, f32[144,128]{1,0:T(8,128)S(1)}, u32[]{:S(2)}, u32[]{:S(2)}) collective-permute-start(f32[144,128]{1,0:T(8,128)S(1)} %add.37), channel_id=1, source_target_pairs={{0,5},{1,8},{2,11},{3,6},{4,13},{5,0},{6,3},{7,14},{8,1},{9,12},{1... | collective-permute-start | bytes 221192 | tf_op jit(solution)/shard_map/ppermute | solution.py:429
  13.5 2.7 %collective-permute-done.2 = f32[144,128]{1,0:T(8,128)S(1)} collective-permute-done((f32[144,128]{1,0:T(8,128)S(1)}, f32[144,128]{1,0:T(8,128)S(1)}, u32[]{:S(2)}, u32[]{:S(2)}) %collective-permute-start.2) | collective-permute-done | bytes 73760 | tf_op jit(solution)/shard_map/ppermute | solution.py:429
  16.3 0.4 collective-permute-start.3
  16.6 3.5 %collective-permute-done.3 = f32[144,128]{1,0:T(8,128)S(1)} collective-permute-done((f32[144,128]{1,0:T(8,128)S(1)}, f32[144,128]{1,0:T(8,128)S(1)}, u32[]{:S(2)}, u32[]{:S(2)}) %collective-permute-start.3) | collective-permute-done | bytes 73760 | tf_op jit(solution)/shard_map/ppermute | solution.py:429
  20.1 0.3 collective-permute-start.4
  20.4 1.0 %collective-permute-done.4.other_ref = f32[144,128]{1,0:T(8,128)S(1)} collective-permute-done((f32[144,128]{1,0:T(8,128)S(1)}, f32[144,128]{1,0:T(8,128)S(1)}, u32[]{:S(2)}, u32[]{:S(2)}) %collective-permute-start.4) | collective-permute-done | bytes 73760 | tf_op jit(solution)/shard_map/ppermute | solution.py:429
  21.4 0.0 copy-done.2
  21.4 0.0 copy-done.1
  21.4 0.0 copy-start
  21.5 0.9 %shard_map.83 = (f32[168,128]{1,0:T(8,128)S(1)}, f32[144,128]{1,0:T(8,128)S(1)}, f32[12,32,128]{2,1,0:T(8,128)S(1)}) custom-call(s32[12]{0:T(128)S(1)} %copy-done.2, f32[12,52,23,128]{3,2,1,0:T(8,128)S(1)} %get-tuple-element.15.cells_ref, f32[12,32,128]{2,1,0:T(8,128)S(1)} %get-tuple-element.16.age_factor_ref, ...), custom_call_target="tpu_custom_call" | custom-call | tf_op jit(solution)/shard_map/pallas_call | solution.py:401
  22.3 0.3 collective-permute-start.5
  22.6 0.3 collective-permute-start.9
  22.9 0.7 %shard_map.84 = (f32[168,128]{1,0:T(8,128)S(1)}, f32[144,128]{1,0:T(8,128)S(1)}) custom-call(s32[12]{0:T(128)S(1)} %copy-done.2, f32[12,52,23,128]{3,2,1,0:T(8,128)S(1)} %get-tuple-element.15.cells_ref, f32[12,32,128]{2,1,0:T(8,128)S(1)} %get-tuple-element.20.factor_ref.scaled_factor_ref, f32[736,128]{1,0:T(8,128)S(1)} %get-tuple-element.17.cross_factor_ref), custom_call_target="tpu_custom_call" | custom-call | tf_op jit(solution)/shard_map/pallas_call | solution.py:401
  23.6 0.0 collective-permute-done.5
  23.7 1.4 %collective-permute-start.6 = (f32[168,128]{1,0:T(8,128)S(1)}, f32[168,128]{1,0:T(8,128)S(1)}, u32[]{:S(2)}, u32[]{:S(2)}) collective-permute-start(f32[168,128]{1,0:T(8,128)S(1)} %add.40), channel_id=1, source_target_pairs={{0,3},{1,4},{2,7},{3,0},{4,1},{5,6},{6,5},{7,2},{8,13},{9,10},{10,... | collective-permute-start | bytes 258056 | tf_op jit(solution)/shard_map/ppermute | solution.py:429
  25.0 0.0 collective-permute-done.9
  25.1 0.5 %collective-permute-start.10 = (f32[144,128]{1,0:T(8,128)S(1)}, f32[144,128]{1,0:T(8,128)S(1)}, u32[]{:S(2)}, u32[]{:S(2)}) collective-permute-start(f32[144,128]{1,0:T(8,128)S(1)} %add.44), channel_id=1, source_target_pairs={{0,3},{1,4},{2,7},{3,0},{4,1},{5,6},{6,5},{7,2},{8,13},{9,10},{10,... | collective-permute-start | bytes 221192 | tf_op jit(solution)/shard_map/ppermute | solution.py:429
  25.6 2.4 %collective-permute-done.6 = f32[168,128]{1,0:T(8,128)S(1)} collective-permute-done((f32[168,128]{1,0:T(8,128)S(1)}, f32[168,128]{1,0:T(8,128)S(1)}, u32[]{:S(2)}, u32[]{:S(2)}) %collective-permute-start.6) | collective-permute-done | bytes 86048 | tf_op jit(solution)/shard_map/ppermute | solution.py:429
  28.0 2.5 %collective-permute-start.7 = (f32[168,128]{1,0:T(8,128)S(1)}, f32[168,128]{1,0:T(8,128)S(1)}, u32[]{:S(2)}, u32[]{:S(2)}) collective-permute-start(f32[168,128]{1,0:T(8,128)S(1)} %add.41), channel_id=1, source_target_pairs={{0,5},{1,8},{2,11},{3,6},{4,13},{5,0},{6,3},{7,14},{8,1},{9,12},{1... | collective-permute-start | bytes 258056 | tf_op jit(solution)/shard_map/ppermute | solution.py:429
  30.5 0.0 collective-permute-done.10
  30.5 0.8 %collective-permute-start.11 = (f32[144,128]{1,0:T(8,128)S(1)}, f32[144,128]{1,0:T(8,128)S(1)}, u32[]{:S(2)}, u32[]{:S(2)}) collective-permute-start(f32[144,128]{1,0:T(8,128)S(1)} %add.45), channel_id=1, source_target_pairs={{0,5},{1,8},{2,11},{3,6},{4,13},{5,0},{6,3},{7,14},{8,1},{9,12},{1... | collective-permute-start | bytes 221192 | tf_op jit(solution)/shard_map/ppermute | solution.py:429
  31.3 2.3 %collective-permute-done.7 = f32[168,128]{1,0:T(8,128)S(1)} collective-permute-done((f32[168,128]{1,0:T(8,128)S(1)}, f32[168,128]{1,0:T(8,128)S(1)}, u32[]{:S(2)}, u32[]{:S(2)}) %collective-permute-start.7) | collective-permute-done | bytes 86048 | tf_op jit(solution)/shard_map/ppermute | solution.py:429
  33.6 0.1 collective-permute-start.8
  33.7 1.6 %collective-permute-done.11 = f32[144,128]{1,0:T(8,128)S(1)} collective-permute-done((f32[144,128]{1,0:T(8,128)S(1)}, f32[144,128]{1,0:T(8,128)S(1)}, u32[]{:S(2)}, u32[]{:S(2)}) %collective-permute-start.11) | collective-permute-done | bytes 73760 | tf_op jit(solution)/shard_map/ppermute | solution.py:429
  35.3 0.4 collective-permute-start.12
  35.7 2.2 %collective-permute-done.8 = f32[168,128]{1,0:T(8,128)S(1)} collective-permute-done((f32[168,128]{1,0:T(8,128)S(1)}, f32[168,128]{1,0:T(8,128)S(1)}, u32[]{:S(2)}, u32[]{:S(2)}) %collective-permute-start.8) | collective-permute-done | bytes 86048 | tf_op jit(solution)/shard_map/ppermute | solution.py:429
  37.9 1.4 %collective-permute-start.13 = (f32[168,128]{1,0:T(8,128)S(1)}, f32[168,128]{1,0:T(8,128)S(1)}, u32[]{:S(2)}, u32[]{:S(2)}) collective-permute-start(f32[168,128]{1,0:T(8,128)S(1)} %add.43.refs_0_), channel_id=1, source_target_pairs={{0,1},{1,0},{2,3},{3,2},{4,5},{5,4},{6,7},{7,6},{8,9},{9,8},{10,11... | collective-permute-start | bytes 258056 | tf_op jit(solution)/shard_map/ppermute | solution.py:429
  39.3 0.0 collective-permute-done.12
  39.3 1.9 %collective-permute-start.14 = (f32[144,128]{1,0:T(8,128)S(1)}, f32[144,128]{1,0:T(8,128)S(1)}, u32[]{:S(2)}, u32[]{:S(2)}) collective-permute-start(f32[144,128]{1,0:T(8,128)S(1)} %add.47.refs_1_), channel_id=1, source_target_pairs={{0,1},{1,0},{2,3},{3,2},{4,5},{5,4},{6,7},{7,6},{8,9},{9,8},{10,11... | collective-permute-start | bytes 221192 | tf_op jit(solution)/shard_map/ppermute | solution.py:429
  41.3 0.9 %collective-permute-done.14.refs_3_ = f32[144,128]{1,0:T(8,128)S(1)} collective-permute-done((f32[144,128]{1,0:T(8,128)S(1)}, f32[144,128]{1,0:T(8,128)S(1)}, u32[]{:S(2)}, u32[]{:S(2)}) %collective-permute-start.14) | collective-permute-done | bytes 73760 | tf_op jit(solution)/shard_map/ppermute | solution.py:429
  42.2 0.0 collective-permute-done.13.refs_2_
  42.2 0.0 copy-done
  42.2 3.2 %shard_map.85 = f32[12,49,23,128]{3,2,1,0:T(8,128)} custom-call(s32[12]{0:T(128)S(1)} %copy-done.2, f32[12,52,23,128]{3,2,1,0:T(8,128)S(1)} %get-tuple-element.15.cells_ref, f32[12,32,128]{2,1,0:T(8,128)S(1)} %get-tuple-element.20.factor_ref.scaled_factor_ref, f32[736,128]{1,0:T(8,128)S(1)} %get-tuple-element.17.cross_factor_ref, f32[24,3136]{1,0:T(8,128)S(1)} %copy-done, ...), custom_call_target="tpu_custom_call" | custom-call | tf_op jit(solution)/shard_map/pallas_call | solution.py:401
  (12 shorter events, 0.1 us)
Async XLA Ops:
  0.0 21.4 %copy-start.2 = (s32[12]{0:T(128)S(1)}, s32[12]{0:T(128)}, u32[]{:S(2)}) copy-start(s32[12]{0:T(128)} %ids_ref.5) | copy-start | bytes 148
  0.0 21.4 %copy-start.1 = (f32[24,1472]{1,0:T(8,128)S(1)}, f32[24,1472]{1,0:T(8,128)}, u32[]{:S(2)}) copy-start(f32[24,1472]{1,0:T(8,128)} %target_ref.2) | copy-start | bytes 423940
  5.4 1.7 %collective-permute-start = (f32[144,128]{1,0:T(8,128)S(1)}, f32[144,128]{1,0:T(8,128)S(1)}, u32[]{:S(2)}, u32[]{:S(2)}) collective-permute-start(f32[144,128]{1,0:T(8,128)S(1)} %get-tuple-element.19), channel_id=1, source_target_pairs={{0,1},{1,0},{2,3},{3,2},{4,5},{5,4},{6,7},{7,6},{8,9},{9,8},{10,11... | collective-permute-start | bytes 221192 | tf_op jit(solution)/shard_map/ppermute | solution.py:429
  7.1 3.8 %collective-permute-start.1 = (f32[144,128]{1,0:T(8,128)S(1)}, f32[144,128]{1,0:T(8,128)S(1)}, u32[]{:S(2)}, u32[]{:S(2)}) collective-permute-start(f32[144,128]{1,0:T(8,128)S(1)} %add.36), channel_id=1, source_target_pairs={{0,3},{1,4},{2,7},{3,0},{4,1},{5,6},{6,5},{7,2},{8,13},{9,10},{10,... | collective-permute-start | bytes 221192 | tf_op jit(solution)/shard_map/ppermute | solution.py:429
  10.9 5.3 %collective-permute-start.2 = (f32[144,128]{1,0:T(8,128)S(1)}, f32[144,128]{1,0:T(8,128)S(1)}, u32[]{:S(2)}, u32[]{:S(2)}) collective-permute-start(f32[144,128]{1,0:T(8,128)S(1)} %add.37), channel_id=1, source_target_pairs={{0,5},{1,8},{2,11},{3,6},{4,13},{5,0},{6,3},{7,14},{8,1},{9,12},{1... | collective-permute-start | bytes 221192 | tf_op jit(solution)/shard_map/ppermute | solution.py:429
  16.3 3.8 %collective-permute-start.3 = (f32[144,128]{1,0:T(8,128)S(1)}, f32[144,128]{1,0:T(8,128)S(1)}, u32[]{:S(2)}, u32[]{:S(2)}) collective-permute-start(f32[144,128]{1,0:T(8,128)S(1)} %add.38), channel_id=1, source_target_pairs={{0,9},{1,2},{2,1},{3,10},{4,7},{5,12},{6,15},{7,4},{8,11},{9,0},{1... | collective-permute-start | bytes 221192 | tf_op jit(solution)/shard_map/ppermute | solution.py:429
  20.1 1.3 %collective-permute-start.4 = (f32[144,128]{1,0:T(8,128)S(1)}, f32[144,128]{1,0:T(8,128)S(1)}, u32[]{:S(2)}, u32[]{:S(2)}) collective-permute-start(f32[144,128]{1,0:T(8,128)S(1)} %add.39.own_ref), channel_id=1, source_target_pairs={{0,1},{1,0},{2,3},{3,2},{4,5},{5,4},{6,7},{7,6},{8,9},{9,8},{10,11... | collective-permute-start | bytes 221192 | tf_op jit(solution)/shard_map/ppermute | solution.py:429
  21.4 20.8 %copy-start = (f32[24,3136]{1,0:T(8,128)S(1)}, f32[24,3136]{1,0:T(8,128)}, u32[]{:S(2)}) copy-start(f32[24,3136]{1,0:T(8,128)} %target_ref.3) | copy-start | bytes 903172
  22.3 1.3 %collective-permute-start.5 = (f32[168,128]{1,0:T(8,128)S(1)}, f32[168,128]{1,0:T(8,128)S(1)}, u32[]{:S(2)}, u32[]{:S(2)}) collective-permute-start(f32[168,128]{1,0:T(8,128)S(1)} %get-tuple-element.22), channel_id=1, source_target_pairs={{0,1},{1,0},{2,3},{3,2},{4,5},{5,4},{6,7},{7,6},{8,9},{9,8},{10,11... | collective-permute-start | bytes 258056 | tf_op jit(solution)/shard_map/ppermute | solution.py:429
  22.6 2.4 %collective-permute-start.9 = (f32[144,128]{1,0:T(8,128)S(1)}, f32[144,128]{1,0:T(8,128)S(1)}, u32[]{:S(2)}, u32[]{:S(2)}) collective-permute-start(f32[144,128]{1,0:T(8,128)S(1)} %get-tuple-element.24), channel_id=1, source_target_pairs={{0,1},{1,0},{2,3},{3,2},{4,5},{5,4},{6,7},{7,6},{8,9},{9,8},{10,11... | collective-permute-start | bytes 221192 | tf_op jit(solution)/shard_map/ppermute | solution.py:429
  23.7 4.3 %collective-permute-start.6 = (f32[168,128]{1,0:T(8,128)S(1)}, f32[168,128]{1,0:T(8,128)S(1)}, u32[]{:S(2)}, u32[]{:S(2)}) collective-permute-start(f32[168,128]{1,0:T(8,128)S(1)} %add.40), channel_id=1, source_target_pairs={{0,3},{1,4},{2,7},{3,0},{4,1},{5,6},{6,5},{7,2},{8,13},{9,10},{10,... | collective-permute-start | bytes 258056 | tf_op jit(solution)/shard_map/ppermute | solution.py:429
  25.1 5.5 %collective-permute-start.10 = (f32[144,128]{1,0:T(8,128)S(1)}, f32[144,128]{1,0:T(8,128)S(1)}, u32[]{:S(2)}, u32[]{:S(2)}) collective-permute-start(f32[144,128]{1,0:T(8,128)S(1)} %add.44), channel_id=1, source_target_pairs={{0,3},{1,4},{2,7},{3,0},{4,1},{5,6},{6,5},{7,2},{8,13},{9,10},{10,... | collective-permute-start | bytes 221192 | tf_op jit(solution)/shard_map/ppermute | solution.py:429
  28.0 5.6 %collective-permute-start.7 = (f32[168,128]{1,0:T(8,128)S(1)}, f32[168,128]{1,0:T(8,128)S(1)}, u32[]{:S(2)}, u32[]{:S(2)}) collective-permute-start(f32[168,128]{1,0:T(8,128)S(1)} %add.41), channel_id=1, source_target_pairs={{0,5},{1,8},{2,11},{3,6},{4,13},{5,0},{6,3},{7,14},{8,1},{9,12},{1... | collective-permute-start | bytes 258056 | tf_op jit(solution)/shard_map/ppermute | solution.py:429
  30.5 4.7 %collective-permute-start.11 = (f32[144,128]{1,0:T(8,128)S(1)}, f32[144,128]{1,0:T(8,128)S(1)}, u32[]{:S(2)}, u32[]{:S(2)}) collective-permute-start(f32[144,128]{1,0:T(8,128)S(1)} %add.45), channel_id=1, source_target_pairs={{0,5},{1,8},{2,11},{3,6},{4,13},{5,0},{6,3},{7,14},{8,1},{9,12},{1... | collective-permute-start | bytes 221192 | tf_op jit(solution)/shard_map/ppermute | solution.py:429
  33.6 4.3 %collective-permute-start.8 = (f32[168,128]{1,0:T(8,128)S(1)}, f32[168,128]{1,0:T(8,128)S(1)}, u32[]{:S(2)}, u32[]{:S(2)}) collective-permute-start(f32[168,128]{1,0:T(8,128)S(1)} %add.42), channel_id=1, source_target_pairs={{0,9},{1,2},{2,1},{3,10},{4,7},{5,12},{6,15},{7,4},{8,11},{9,0},{1... | collective-permute-start | bytes 258056 | tf_op jit(solution)/shard_map/ppermute | solution.py:429
  35.3 4.0 %collective-permute-start.12 = (f32[144,128]{1,0:T(8,128)S(1)}, f32[144,128]{1,0:T(8,128)S(1)}, u32[]{:S(2)}, u32[]{:S(2)}) collective-permute-start(f32[144,128]{1,0:T(8,128)S(1)} %add.46), channel_id=1, source_target_pairs={{0,9},{1,2},{2,1},{3,10},{4,7},{5,12},{6,15},{7,4},{8,11},{9,0},{1... | collective-permute-start | bytes 221192 | tf_op jit(solution)/shard_map/ppermute | solution.py:429
  37.9 4.3 %collective-permute-start.13 = (f32[168,128]{1,0:T(8,128)S(1)}, f32[168,128]{1,0:T(8,128)S(1)}, u32[]{:S(2)}, u32[]{:S(2)}) collective-permute-start(f32[168,128]{1,0:T(8,128)S(1)} %add.43.refs_0_), channel_id=1, source_target_pairs={{0,1},{1,0},{2,3},{3,2},{4,5},{5,4},{6,7},{7,6},{8,9},{9,8},{10,11... | collective-permute-start | bytes 258056 | tf_op jit(solution)/shard_map/ppermute | solution.py:429
  39.3 2.9 %collective-permute-start.14 = (f32[144,128]{1,0:T(8,128)S(1)}, f32[144,128]{1,0:T(8,128)S(1)}, u32[]{:S(2)}, u32[]{:S(2)}) collective-permute-start(f32[144,128]{1,0:T(8,128)S(1)} %add.47.refs_1_), channel_id=1, source_target_pairs={{0,1},{1,0},{2,3},{3,2},{4,5},{5,4},{6,7},{7,6},{8,9},{9,8},{10,11... | collective-permute-start | bytes 221192 | tf_op jit(solution)/shard_map/ppermute | solution.py:429
where the time goes:
time: 45.6 us; the launch traced here: 45.4 us
  waiting for transfers between devices  20.9 us (46%)
  starting transfers between devices  14.1 us (31%)
  Pallas kernels  10.2 us (22%)
    ppermute x15, waiting for transfers between devices, swap(): return lax.ppermute(x, 'tract', [(i, partner(i)) for i in range(devices)])  20.9 us
    ppermute x15, starting transfers between devices, swap(): return lax.ppermute(x, 'tract', [(i, partner(i)) for i in range(devices)])  14.1 us
    pallas_call x4, Pallas kernels, placed(): return run(*map(pltpu.with_memory_space_constraint, args, in_spaces))  10.2 us
  transfers between devices with their start and end apart: 15, of which 10 were waited for; matrix products, arithmetic and copies ran while one was open for 0% of the time, Pallas kernels for 2%

commit v1 on v0

--- a/solution.py
+++ b/solution.py
@@ -159,6 +159,8 @@
     rows_ref[...] = jnp.zeros(rows_ref.shape, F32)
     for copy in small:
         copy.wait()
+    for t in range(FIRST, tracts):
+        table_copy(t).start()
     for source_ref, target_ref, rows, mask in (
         (age_sex_ref, age_target_ref, ages, sex0),
         (race_hisp_ref, race_target_ref, races, hisp0),
@@ -169,9 +171,6 @@
             target_ref[t, 0:rows] = jnp.where(
                 mask, column_of(row, rows, 2, 0), column_of(row, rows, 2, 1)
             )
-
-    for t in range(FIRST, tracts):
-        table_copy(t).start()
 
     def group_sums(values, mask):
         first = [masked_lane_sum(x, mask) for x in values]

time: 45.6 us -> 45.5 us (level)
  no operation moved by 1% of the time
where the time goes in v1:
time: 45.5 us; the launch traced here: 45.4 us
  waiting for transfers between devices  20.9 us (46%)
  starting transfers between devices  14.1 us (31%)
  Pallas kernels  10.2 us (22%)
    ppermute x15, waiting for transfers between devices, swap(): return lax.ppermute(x, 'tract', [(i, partner(i)) for i in range(devices)])  20.9 us
    ppermute x15, starting transfers between devices, swap(): return lax.ppermute(x, 'tract', [(i, partner(i)) for i in range(devices)])  14.1 us
    pallas_call x4, Pallas kernels, placed(): return run(*map(pltpu.with_memory_space_constraint, args, in_spaces))  10.2 us
  transfers between devices with their start and end apart: 15, of which 10 were waited for; matrix products, arithmetic and copies ran while one was open for 0% of the time, Pallas kernels for 2%

profile of v1, /device:TPU:13, one launch (start us, length us, event | category | flops | bytes accessed | tf_op | source)
XLA Modules:
  0.0 45.4 jit_solution(5218843595648113140)
XLA Ops:
  0.0 0.0 copy-start.2
  0.0 0.0 copy-start.1
  0.0 5.4 %shard_map.82 = (f32[144,128]{1,0:T(8,128)S(1)}, f32[144,128]{1,0:T(8,128)S(1)}, f32[12,32,128]{2,1,0:T(8,128)S(1)}, f32[736,128]{1,0:T(8,128)S(1)}, f32[12,52,23,128]{3,2,1,0:T(8,128)S(1)}) custom-call(s32[12]{0:T(128)} %ids_ref.5, f32[12,49,23,128]{3,2,1,0:T(8,128)} %bitcast.6, f32[12,46]{1,0:T(8,128)} %age_sex_hbm.1, f32[12,14]{1,0:T(8,128)} %race_hisp_hbm.1, ...), custom_call_target="tpu_custom_call" | custom-call | tf_op jit(solution)/shard_map/pallas_call | solution.py:400
  5.4 0.7 %collective-permute-start = (f32[144,128]{1,0:T(8,128)S(1)}, f32[144,128]{1,0:T(8,128)S(1)}, u32[]{:S(2)}, u32[]{:S(2)}) collective-permute-start(f32[144,128]{1,0:T(8,128)S(1)} %get-tuple-element.19), channel_id=1, source_target_pairs={{0,1},{1,0},{2,3},{3,2},{4,5},{5,4},{6,7},{7,6},{8,9},{9,8},{10,11... | collective-permute-start | bytes 221192 | tf_op jit(solution)/shard_map/ppermute | solution.py:428
  6.1 0.9 %collective-permute-done = f32[144,128]{1,0:T(8,128)S(1)} collective-permute-done((f32[144,128]{1,0:T(8,128)S(1)}, f32[144,128]{1,0:T(8,128)S(1)}, u32[]{:S(2)}, u32[]{:S(2)}) %collective-permute-start) | collective-permute-done | bytes 73760 | tf_op jit(solution)/shard_map/ppermute | solution.py:428
  7.1 0.5 %collective-permute-start.1 = (f32[144,128]{1,0:T(8,128)S(1)}, f32[144,128]{1,0:T(8,128)S(1)}, u32[]{:S(2)}, u32[]{:S(2)}) collective-permute-start(f32[144,128]{1,0:T(8,128)S(1)} %add.36), channel_id=1, source_target_pairs={{0,3},{1,4},{2,7},{3,0},{4,1},{5,6},{6,5},{7,2},{8,13},{9,10},{10,... | collective-permute-start | bytes 221192 | tf_op jit(solution)/shard_map/ppermute | solution.py:428
  7.5 3.4 %collective-permute-done.1 = f32[144,128]{1,0:T(8,128)S(1)} collective-permute-done((f32[144,128]{1,0:T(8,128)S(1)}, f32[144,128]{1,0:T(8,128)S(1)}, u32[]{:S(2)}, u32[]{:S(2)}) %collective-permute-start.1) | collective-permute-done | bytes 73760 | tf_op jit(solution)/shard_map/ppermute | solution.py:428
  10.9 2.6 %collective-permute-start.2 = (f32[144,128]{1,0:T(8,128)S(1)}, f32[144,128]{1,0:T(8,128)S(1)}, u32[]{:S(2)}, u32[]{:S(2)}) collective-permute-start(f32[144,128]{1,0:T(8,128)S(1)} %add.37), channel_id=1, source_target_pairs={{0,5},{1,8},{2,11},{3,6},{4,13},{5,0},{6,3},{7,14},{8,1},{9,12},{1... | collective-permute-start | bytes 221192 | tf_op jit(solution)/shard_map/ppermute | solution.py:428
  13.5 2.7 %collective-permute-done.2 = f32[144,128]{1,0:T(8,128)S(1)} collective-permute-done((f32[144,128]{1,0:T(8,128)S(1)}, f32[144,128]{1,0:T(8,128)S(1)}, u32[]{:S(2)}, u32[]{:S(2)}) %collective-permute-start.2) | collective-permute-done | bytes 73760 | tf_op jit(solution)/shard_map/ppermute | solution.py:428
  16.3 0.4 collective-permute-start.3
  16.6 3.5 %collective-permute-done.3 = f32[144,128]{1,0:T(8,128)S(1)} collective-permute-done((f32[144,128]{1,0:T(8,128)S(1)}, f32[144,128]{1,0:T(8,128)S(1)}, u32[]{:S(2)}, u32[]{:S(2)}) %collective-permute-start.3) | collective-permute-done | bytes 73760 | tf_op jit(solution)/shard_map/ppermute | solution.py:428
  20.1 0.3 collective-permute-start.4
  20.4 1.0 %collective-permute-done.4.other_ref = f32[144,128]{1,0:T(8,128)S(1)} collective-permute-done((f32[144,128]{1,0:T(8,128)S(1)}, f32[144,128]{1,0:T(8,128)S(1)}, u32[]{:S(2)}, u32[]{:S(2)}) %collective-permute-start.4) | collective-permute-done | bytes 73760 | tf_op jit(solution)/shard_map/ppermute | solution.py:428
  21.4 0.0 copy-done.2
  21.4 0.0 copy-done.1
  21.4 0.0 copy-start
  21.5 0.9 %shard_map.83 = (f32[168,128]{1,0:T(8,128)S(1)}, f32[144,128]{1,0:T(8,128)S(1)}, f32[12,32,128]{2,1,0:T(8,128)S(1)}) custom-call(s32[12]{0:T(128)S(1)} %copy-done.2, f32[12,52,23,128]{3,2,1,0:T(8,128)S(1)} %get-tuple-element.15.cells_ref, f32[12,32,128]{2,1,0:T(8,128)S(1)} %get-tuple-element.16.age_factor_ref, ...), custom_call_target="tpu_custom_call" | custom-call | tf_op jit(solution)/shard_map/pallas_call | solution.py:400
  22.3 0.3 collective-permute-start.5
  22.6 0.3 collective-permute-start.9
  22.9 0.7 %shard_map.84 = (f32[168,128]{1,0:T(8,128)S(1)}, f32[144,128]{1,0:T(8,128)S(1)}) custom-call(s32[12]{0:T(128)S(1)} %copy-done.2, f32[12,52,23,128]{3,2,1,0:T(8,128)S(1)} %get-tuple-element.15.cells_ref, f32[12,32,128]{2,1,0:T(8,128)S(1)} %get-tuple-element.20.factor_ref.scaled_factor_ref, f32[736,128]{1,0:T(8,128)S(1)} %get-tuple-element.17.cross_factor_ref), custom_call_target="tpu_custom_call" | custom-call | tf_op jit(solution)/shard_map/pallas_call | solution.py:400
  23.6 0.0 collective-permute-done.5
  23.7 1.4 %collective-permute-start.6 = (f32[168,128]{1,0:T(8,128)S(1)}, f32[168,128]{1,0:T(8,128)S(1)}, u32[]{:S(2)}, u32[]{:S(2)}) collective-permute-start(f32[168,128]{1,0:T(8,128)S(1)} %add.40), channel_id=1, source_target_pairs={{0,3},{1,4},{2,7},{3,0},{4,1},{5,6},{6,5},{7,2},{8,13},{9,10},{10,... | collective-permute-start | bytes 258056 | tf_op jit(solution)/shard_map/ppermute | solution.py:428
  25.0 0.0 collective-permute-done.9
  25.1 0.5 %collective-permute-start.10 = (f32[144,128]{1,0:T(8,128)S(1)}, f32[144,128]{1,0:T(8,128)S(1)}, u32[]{:S(2)}, u32[]{:S(2)}) collective-permute-start(f32[144,128]{1,0:T(8,128)S(1)} %add.44), channel_id=1, source_target_pairs={{0,3},{1,4},{2,7},{3,0},{4,1},{5,6},{6,5},{7,2},{8,13},{9,10},{10,... | collective-permute-start | bytes 221192 | tf_op jit(solution)/shard_map/ppermute | solution.py:428
  25.6 2.4 %collective-permute-done.6 = f32[168,128]{1,0:T(8,128)S(1)} collective-permute-done((f32[168,128]{1,0:T(8,128)S(1)}, f32[168,128]{1,0:T(8,128)S(1)}, u32[]{:S(2)}, u32[]{:S(2)}) %collective-permute-start.6) | collective-permute-done | bytes 86048 | tf_op jit(solution)/shard_map/ppermute | solution.py:428
  28.0 2.5 %collective-permute-start.7 = (f32[168,128]{1,0:T(8,128)S(1)}, f32[168,128]{1,0:T(8,128)S(1)}, u32[]{:S(2)}, u32[]{:S(2)}) collective-permute-start(f32[168,128]{1,0:T(8,128)S(1)} %add.41), channel_id=1, source_target_pairs={{0,5},{1,8},{2,11},{3,6},{4,13},{5,0},{6,3},{7,14},{8,1},{9,12},{1... | collective-permute-start | bytes 258056 | tf_op jit(solution)/shard_map/ppermute | solution.py:428
  30.5 0.0 collective-permute-done.10
  30.5 0.8 %collective-permute-start.11 = (f32[144,128]{1,0:T(8,128)S(1)}, f32[144,128]{1,0:T(8,128)S(1)}, u32[]{:S(2)}, u32[]{:S(2)}) collective-permute-start(f32[144,128]{1,0:T(8,128)S(1)} %add.45), channel_id=1, source_target_pairs={{0,5},{1,8},{2,11},{3,6},{4,13},{5,0},{6,3},{7,14},{8,1},{9,12},{1... | collective-permute-start | bytes 221192 | tf_op jit(solution)/shard_map/ppermute | solution.py:428
  31.3 2.3 %collective-permute-done.7 = f32[168,128]{1,0:T(8,128)S(1)} collective-permute-done((f32[168,128]{1,0:T(8,128)S(1)}, f32[168,128]{1,0:T(8,128)S(1)}, u32[]{:S(2)}, u32[]{:S(2)}) %collective-permute-start.7) | collective-permute-done | bytes 86048 | tf_op jit(solution)/shard_map/ppermute | solution.py:428
  33.6 0.1 collective-permute-start.8
  33.7 1.6 %collective-permute-done.11 = f32[144,128]{1,0:T(8,128)S(1)} collective-permute-done((f32[144,128]{1,0:T(8,128)S(1)}, f32[144,128]{1,0:T(8,128)S(1)}, u32[]{:S(2)}, u32[]{:S(2)}) %collective-permute-start.11) | collective-permute-done | bytes 73760 | tf_op jit(solution)/shard_map/ppermute | solution.py:428
  35.3 0.4 collective-permute-start.12
  35.7 2.2 %collective-permute-done.8 = f32[168,128]{1,0:T(8,128)S(1)} collective-permute-done((f32[168,128]{1,0:T(8,128)S(1)}, f32[168,128]{1,0:T(8,128)S(1)}, u32[]{:S(2)}, u32[]{:S(2)}) %collective-permute-start.8) | collective-permute-done | bytes 86048 | tf_op jit(solution)/shard_map/ppermute | solution.py:428
  37.9 1.4 %collective-permute-start.13 = (f32[168,128]{1,0:T(8,128)S(1)}, f32[168,128]{1,0:T(8,128)S(1)}, u32[]{:S(2)}, u32[]{:S(2)}) collective-permute-start(f32[168,128]{1,0:T(8,128)S(1)} %add.43.refs_0_), channel_id=1, source_target_pairs={{0,1},{1,0},{2,3},{3,2},{4,5},{5,4},{6,7},{7,6},{8,9},{9,8},{10,11... | collective-permute-start | bytes 258056 | tf_op jit(solution)/shard_map/ppermute | solution.py:428
  39.3 0.0 collective-permute-done.12
  39.3 1.9 %collective-permute-start.14 = (f32[144,128]{1,0:T(8,128)S(1)}, f32[144,128]{1,0:T(8,128)S(1)}, u32[]{:S(2)}, u32[]{:S(2)}) collective-permute-start(f32[144,128]{1,0:T(8,128)S(1)} %add.47.refs_1_), channel_id=1, source_target_pairs={{0,1},{1,0},{2,3},{3,2},{4,5},{5,4},{6,7},{7,6},{8,9},{9,8},{10,11... | collective-permute-start | bytes 221192 | tf_op jit(solution)/shard_map/ppermute | solution.py:428
  41.3 0.9 %collective-permute-done.14.refs_3_ = f32[144,128]{1,0:T(8,128)S(1)} collective-permute-done((f32[144,128]{1,0:T(8,128)S(1)}, f32[144,128]{1,0:T(8,128)S(1)}, u32[]{:S(2)}, u32[]{:S(2)}) %collective-permute-start.14) | collective-permute-done | bytes 73760 | tf_op jit(solution)/shard_map/ppermute | solution.py:428
  42.2 0.0 collective-permute-done.13.refs_2_
  42.2 0.0 copy-done
  42.2 3.2 %shard_map.85 = f32[12,49,23,128]{3,2,1,0:T(8,128)} custom-call(s32[12]{0:T(128)S(1)} %copy-done.2, f32[12,52,23,128]{3,2,1,0:T(8,128)S(1)} %get-tuple-element.15.cells_ref, f32[12,32,128]{2,1,0:T(8,128)S(1)} %get-tuple-element.20.factor_ref.scaled_factor_ref, f32[736,128]{1,0:T(8,128)S(1)} %get-tuple-element.17.cross_factor_ref, f32[24,3136]{1,0:T(8,128)S(1)} %copy-done, ...), custom_call_target="tpu_custom_call" | custom-call | tf_op jit(solution)/shard_map/pallas_call | solution.py:400
  (12 shorter events, 0.1 us)
Async XLA Ops:
  0.0 21.4 %copy-start.2 = (s32[12]{0:T(128)S(1)}, s32[12]{0:T(128)}, u32[]{:S(2)}) copy-start(s32[12]{0:T(128)} %ids_ref.5) | copy-start | bytes 148
  0.0 21.4 %copy-start.1 = (f32[24,1472]{1,0:T(8,128)S(1)}, f32[24,1472]{1,0:T(8,128)}, u32[]{:S(2)}) copy-start(f32[24,1472]{1,0:T(8,128)} %target_ref.2) | copy-start | bytes 423940
  5.4 1.7 %collective-permute-start = (f32[144,128]{1,0:T(8,128)S(1)}, f32[144,128]{1,0:T(8,128)S(1)}, u32[]{:S(2)}, u32[]{:S(2)}) collective-permute-start(f32[144,128]{1,0:T(8,128)S(1)} %get-tuple-element.19), channel_id=1, source_target_pairs={{0,1},{1,0},{2,3},{3,2},{4,5},{5,4},{6,7},{7,6},{8,9},{9,8},{10,11... | collective-permute-start | bytes 221192 | tf_op jit(solution)/shard_map/ppermute | solution.py:428
  7.1 3.8 %collective-permute-start.1 = (f32[144,128]{1,0:T(8,128)S(1)}, f32[144,128]{1,0:T(8,128)S(1)}, u32[]{:S(2)}, u32[]{:S(2)}) collective-permute-start(f32[144,128]{1,0:T(8,128)S(1)} %add.36), channel_id=1, source_target_pairs={{0,3},{1,4},{2,7},{3,0},{4,1},{5,6},{6,5},{7,2},{8,13},{9,10},{10,... | collective-permute-start | bytes 221192 | tf_op jit(solution)/shard_map/ppermute | solution.py:428
  10.9 5.3 %collective-permute-start.2 = (f32[144,128]{1,0:T(8,128)S(1)}, f32[144,128]{1,0:T(8,128)S(1)}, u32[]{:S(2)}, u32[]{:S(2)}) collective-permute-start(f32[144,128]{1,0:T(8,128)S(1)} %add.37), channel_id=1, source_target_pairs={{0,5},{1,8},{2,11},{3,6},{4,13},{5,0},{6,3},{7,14},{8,1},{9,12},{1... | collective-permute-start | bytes 221192 | tf_op jit(solution)/shard_map/ppermute | solution.py:428
  16.3 3.8 %collective-permute-start.3 = (f32[144,128]{1,0:T(8,128)S(1)}, f32[144,128]{1,0:T(8,128)S(1)}, u32[]{:S(2)}, u32[]{:S(2)}) collective-permute-start(f32[144,128]{1,0:T(8,128)S(1)} %add.38), channel_id=1, source_target_pairs={{0,9},{1,2},{2,1},{3,10},{4,7},{5,12},{6,15},{7,4},{8,11},{9,0},{1... | collective-permute-start | bytes 221192 | tf_op jit(solution)/shard_map/ppermute | solution.py:428
  20.1 1.3 %collective-permute-start.4 = (f32[144,128]{1,0:T(8,128)S(1)}, f32[144,128]{1,0:T(8,128)S(1)}, u32[]{:S(2)}, u32[]{:S(2)}) collective-permute-start(f32[144,128]{1,0:T(8,128)S(1)} %add.39.own_ref), channel_id=1, source_target_pairs={{0,1},{1,0},{2,3},{3,2},{4,5},{5,4},{6,7},{7,6},{8,9},{9,8},{10,11... | collective-permute-start | bytes 221192 | tf_op jit(solution)/shard_map/ppermute | solution.py:428
  21.4 20.8 %copy-start = (f32[24,3136]{1,0:T(8,128)S(1)}, f32[24,3136]{1,0:T(8,128)}, u32[]{:S(2)}) copy-start(f32[24,3136]{1,0:T(8,128)} %target_ref.3) | copy-start | bytes 903172
  22.3 1.3 %collective-permute-start.5 = (f32[168,128]{1,0:T(8,128)S(1)}, f32[168,128]{1,0:T(8,128)S(1)}, u32[]{:S(2)}, u32[]{:S(2)}) collective-permute-start(f32[168,128]{1,0:T(8,128)S(1)} %get-tuple-element.22), channel_id=1, source_target_pairs={{0,1},{1,0},{2,3},{3,2},{4,5},{5,4},{6,7},{7,6},{8,9},{9,8},{10,11... | collective-permute-start | bytes 258056 | tf_op jit(solution)/shard_map/ppermute | solution.py:428
  22.6 2.4 %collective-permute-start.9 = (f32[144,128]{1,0:T(8,128)S(1)}, f32[144,128]{1,0:T(8,128)S(1)}, u32[]{:S(2)}, u32[]{:S(2)}) collective-permute-start(f32[144,128]{1,0:T(8,128)S(1)} %get-tuple-element.24), channel_id=1, source_target_pairs={{0,1},{1,0},{2,3},{3,2},{4,5},{5,4},{6,7},{7,6},{8,9},{9,8},{10,11... | collective-permute-start | bytes 221192 | tf_op jit(solution)/shard_map/ppermute | solution.py:428
  23.7 4.3 %collective-permute-start.6 = (f32[168,128]{1,0:T(8,128)S(1)}, f32[168,128]{1,0:T(8,128)S(1)}, u32[]{:S(2)}, u32[]{:S(2)}) collective-permute-start(f32[168,128]{1,0:T(8,128)S(1)} %add.40), channel_id=1, source_target_pairs={{0,3},{1,4},{2,7},{3,0},{4,1},{5,6},{6,5},{7,2},{8,13},{9,10},{10,... | collective-permute-start | bytes 258056 | tf_op jit(solution)/shard_map/ppermute | solution.py:428
  25.1 5.5 %collective-permute-start.10 = (f32[144,128]{1,0:T(8,128)S(1)}, f32[144,128]{1,0:T(8,128)S(1)}, u32[]{:S(2)}, u32[]{:S(2)}) collective-permute-start(f32[144,128]{1,0:T(8,128)S(1)} %add.44), channel_id=1, source_target_pairs={{0,3},{1,4},{2,7},{3,0},{4,1},{5,6},{6,5},{7,2},{8,13},{9,10},{10,... | collective-permute-start | bytes 221192 | tf_op jit(solution)/shard_map/ppermute | solution.py:428
  28.0 5.6 %collective-permute-start.7 = (f32[168,128]{1,0:T(8,128)S(1)}, f32[168,128]{1,0:T(8,128)S(1)}, u32[]{:S(2)}, u32[]{:S(2)}) collective-permute-start(f32[168,128]{1,0:T(8,128)S(1)} %add.41), channel_id=1, source_target_pairs={{0,5},{1,8},{2,11},{3,6},{4,13},{5,0},{6,3},{7,14},{8,1},{9,12},{1... | collective-permute-start | bytes 258056 | tf_op jit(solution)/shard_map/ppermute | solution.py:428
  30.5 4.7 %collective-permute-start.11 = (f32[144,128]{1,0:T(8,128)S(1)}, f32[144,128]{1,0:T(8,128)S(1)}, u32[]{:S(2)}, u32[]{:S(2)}) collective-permute-start(f32[144,128]{1,0:T(8,128)S(1)} %add.45), channel_id=1, source_target_pairs={{0,5},{1,8},{2,11},{3,6},{4,13},{5,0},{6,3},{7,14},{8,1},{9,12},{1... | collective-permute-start | bytes 221192 | tf_op jit(solution)/shard_map/ppermute | solution.py:428
  33.6 4.3 %collective-permute-start.8 = (f32[168,128]{1,0:T(8,128)S(1)}, f32[168,128]{1,0:T(8,128)S(1)}, u32[]{:S(2)}, u32[]{:S(2)}) collective-permute-start(f32[168,128]{1,0:T(8,128)S(1)} %add.42), channel_id=1, source_target_pairs={{0,9},{1,2},{2,1},{3,10},{4,7},{5,12},{6,15},{7,4},{8,11},{9,0},{1... | collective-permute-start | bytes 258056 | tf_op jit(solution)/shard_map/ppermute | solution.py:428
  35.3 4.0 %collective-permute-start.12 = (f32[144,128]{1,0:T(8,128)S(1)}, f32[144,128]{1,0:T(8,128)S(1)}, u32[]{:S(2)}, u32[]{:S(2)}) collective-permute-start(f32[144,128]{1,0:T(8,128)S(1)} %add.46), channel_id=1, source_target_pairs={{0,9},{1,2},{2,1},{3,10},{4,7},{5,12},{6,15},{7,4},{8,11},{9,0},{1... | collective-permute-start | bytes 221192 | tf_op jit(solution)/shard_map/ppermute | solution.py:428
  37.9 4.3 %collective-permute-start.13 = (f32[168,128]{1,0:T(8,128)S(1)}, f32[168,128]{1,0:T(8,128)S(1)}, u32[]{:S(2)}, u32[]{:S(2)}) collective-permute-start(f32[168,128]{1,0:T(8,128)S(1)} %add.43.refs_0_), channel_id=1, source_target_pairs={{0,1},{1,0},{2,3},{3,2},{4,5},{5,4},{6,7},{7,6},{8,9},{9,8},{10,11... | collective-permute-start | bytes 258056 | tf_op jit(solution)/shard_map/ppermute | solution.py:428
  39.3 2.9 %collective-permute-start.14 = (f32[144,128]{1,0:T(8,128)S(1)}, f32[144,128]{1,0:T(8,128)S(1)}, u32[]{:S(2)}, u32[]{:S(2)}) collective-permute-start(f32[144,128]{1,0:T(8,128)S(1)} %add.47.refs_1_), channel_id=1, source_target_pairs={{0,1},{1,0},{2,3},{3,2},{4,5},{5,4},{6,7},{7,6},{8,9},{9,8},{10,11... | collective-permute-start | bytes 221192 | tf_op jit(solution)/shard_map/ppermute | solution.py:428

commit v2 on v1

--- a/solution.py
+++ b/solution.py
@@ -253,7 +253,6 @@
         each(group.start, group.stop, add_ages)
         small_steps(group)
         each(group.start, group.stop, add_scaled)
-        pack(group)
 
     before = None
     for start in range(0, tracts, GROUP):
@@ -262,6 +261,7 @@
         before = range(start, min(start + GROUP, tracts))
         each(before.start, before.stop, arrive, 1)
     work(before)
+    pack(range(tracts))
     put_halves(rows_ref, [keep_ref], [send_ref])
 
 

time: 45.5 us -> 45.5 us (level)
  no operation moved by 1% of the time
where the time goes in v2:
time: 45.5 us; the launch traced here: 45.4 us
  waiting for transfers between devices  20.8 us (46%)
  starting transfers between devices  14.1 us (31%)
  Pallas kernels  10.2 us (22%)
    ppermute x15, waiting for transfers between devices, swap(): return lax.ppermute(x, 'tract', [(i, partner(i)) for i in range(devices)])  20.8 us
    ppermute x15, starting transfers between devices, swap(): return lax.ppermute(x, 'tract', [(i, partner(i)) for i in range(devices)])  14.1 us
    pallas_call x4, Pallas kernels, placed(): return run(*map(pltpu.with_memory_space_constraint, args, in_spaces))  10.2 us
  transfers between devices with their start and end apart: 15, of which 10 were waited for; matrix products, arithmetic and copies ran while one was open for 0% of the time, Pallas kernels for 2%

profile of v2, /device:TPU:13, one launch (start us, length us, event | category | flops | bytes accessed | tf_op | source)
XLA Modules:
  0.0 45.4 jit_solution(9408149400521357919)
XLA Ops:
  0.0 0.0 copy-start.2
  0.0 0.0 copy-start.1
  0.0 5.4 %shard_map.82 = (f32[144,128]{1,0:T(8,128)S(1)}, f32[144,128]{1,0:T(8,128)S(1)}, f32[12,32,128]{2,1,0:T(8,128)S(1)}, f32[736,128]{1,0:T(8,128)S(1)}, f32[12,52,23,128]{3,2,1,0:T(8,128)S(1)}) custom-call(s32[12]{0:T(128)} %ids_ref.5, f32[12,49,23,128]{3,2,1,0:T(8,128)} %bitcast.6, f32[12,46]{1,0:T(8,128)} %age_sex_hbm.1, f32[12,14]{1,0:T(8,128)} %race_hisp_hbm.1, ...), custom_call_target="tpu_custom_call" | custom-call | tf_op jit(solution)/shard_map/pallas_call | solution.py:400
  5.4 0.7 %collective-permute-start = (f32[144,128]{1,0:T(8,128)S(1)}, f32[144,128]{1,0:T(8,128)S(1)}, u32[]{:S(2)}, u32[]{:S(2)}) collective-permute-start(f32[144,128]{1,0:T(8,128)S(1)} %get-tuple-element.19), channel_id=1, source_target_pairs={{0,1},{1,0},{2,3},{3,2},{4,5},{5,4},{6,7},{7,6},{8,9},{9,8},{10,11... | collective-permute-start | bytes 221192 | tf_op jit(solution)/shard_map/ppermute | solution.py:428
  6.1 0.9 %collective-permute-done = f32[144,128]{1,0:T(8,128)S(1)} collective-permute-done((f32[144,128]{1,0:T(8,128)S(1)}, f32[144,128]{1,0:T(8,128)S(1)}, u32[]{:S(2)}, u32[]{:S(2)}) %collective-permute-start) | collective-permute-done | bytes 73760 | tf_op jit(solution)/shard_map/ppermute | solution.py:428
  7.1 0.5 %collective-permute-start.1 = (f32[144,128]{1,0:T(8,128)S(1)}, f32[144,128]{1,0:T(8,128)S(1)}, u32[]{:S(2)}, u32[]{:S(2)}) collective-permute-start(f32[144,128]{1,0:T(8,128)S(1)} %add.36), channel_id=1, source_target_pairs={{0,3},{1,4},{2,7},{3,0},{4,1},{5,6},{6,5},{7,2},{8,13},{9,10},{10,... | collective-permute-start | bytes 221192 | tf_op jit(solution)/shard_map/ppermute | solution.py:428
  7.5 3.4 %collective-permute-done.1 = f32[144,128]{1,0:T(8,128)S(1)} collective-permute-done((f32[144,128]{1,0:T(8,128)S(1)}, f32[144,128]{1,0:T(8,128)S(1)}, u32[]{:S(2)}, u32[]{:S(2)}) %collective-permute-start.1) | collective-permute-done | bytes 73760 | tf_op jit(solution)/shard_map/ppermute | solution.py:428
  10.9 2.6 %collective-permute-start.2 = (f32[144,128]{1,0:T(8,128)S(1)}, f32[144,128]{1,0:T(8,128)S(1)}, u32[]{:S(2)}, u32[]{:S(2)}) collective-permute-start(f32[144,128]{1,0:T(8,128)S(1)} %add.37), channel_id=1, source_target_pairs={{0,5},{1,8},{2,11},{3,6},{4,13},{5,0},{6,3},{7,14},{8,1},{9,12},{1... | collective-permute-start | bytes 221192 | tf_op jit(solution)/shard_map/ppermute | solution.py:428
  13.5 2.7 %collective-permute-done.2 = f32[144,128]{1,0:T(8,128)S(1)} collective-permute-done((f32[144,128]{1,0:T(8,128)S(1)}, f32[144,128]{1,0:T(8,128)S(1)}, u32[]{:S(2)}, u32[]{:S(2)}) %collective-permute-start.2) | collective-permute-done | bytes 73760 | tf_op jit(solution)/shard_map/ppermute | solution.py:428
  16.2 0.4 collective-permute-start.3
  16.6 3.5 %collective-permute-done.3 = f32[144,128]{1,0:T(8,128)S(1)} collective-permute-done((f32[144,128]{1,0:T(8,128)S(1)}, f32[144,128]{1,0:T(8,128)S(1)}, u32[]{:S(2)}, u32[]{:S(2)}) %collective-permute-start.3) | collective-permute-done | bytes 73760 | tf_op jit(solution)/shard_map/ppermute | solution.py:428
  20.1 0.3 collective-permute-start.4
  20.4 1.0 %collective-permute-done.4.other_ref = f32[144,128]{1,0:T(8,128)S(1)} collective-permute-done((f32[144,128]{1,0:T(8,128)S(1)}, f32[144,128]{1,0:T(8,128)S(1)}, u32[]{:S(2)}, u32[]{:S(2)}) %collective-permute-start.4) | collective-permute-done | bytes 73760 | tf_op jit(solution)/shard_map/ppermute | solution.py:428
  21.4 0.0 copy-done.2
  21.4 0.0 copy-done.1
  21.4 0.0 copy-start
  21.4 0.9 %shard_map.83 = (f32[168,128]{1,0:T(8,128)S(1)}, f32[144,128]{1,0:T(8,128)S(1)}, f32[12,32,128]{2,1,0:T(8,128)S(1)}) custom-call(s32[12]{0:T(128)S(1)} %copy-done.2, f32[12,52,23,128]{3,2,1,0:T(8,128)S(1)} %get-tuple-element.15.cells_ref, f32[12,32,128]{2,1,0:T(8,128)S(1)} %get-tuple-element.16.age_factor_ref, ...), custom_call_target="tpu_custom_call" | custom-call | tf_op jit(solution)/shard_map/pallas_call | solution.py:400
  22.3 0.3 collective-permute-start.5
  22.6 0.3 collective-permute-start.9
  22.9 0.7 %shard_map.84 = (f32[168,128]{1,0:T(8,128)S(1)}, f32[144,128]{1,0:T(8,128)S(1)}) custom-call(s32[12]{0:T(128)S(1)} %copy-done.2, f32[12,52,23,128]{3,2,1,0:T(8,128)S(1)} %get-tuple-element.15.cells_ref, f32[12,32,128]{2,1,0:T(8,128)S(1)} %get-tuple-element.20.factor_ref.scaled_factor_ref, f32[736,128]{1,0:T(8,128)S(1)} %get-tuple-element.17.cross_factor_ref), custom_call_target="tpu_custom_call" | custom-call | tf_op jit(solution)/shard_map/pallas_call | solution.py:400
  23.6 0.0 collective-permute-done.5
  23.7 1.4 %collective-permute-start.6 = (f32[168,128]{1,0:T(8,128)S(1)}, f32[168,128]{1,0:T(8,128)S(1)}, u32[]{:S(2)}, u32[]{:S(2)}) collective-permute-start(f32[168,128]{1,0:T(8,128)S(1)} %add.40), channel_id=1, source_target_pairs={{0,3},{1,4},{2,7},{3,0},{4,1},{5,6},{6,5},{7,2},{8,13},{9,10},{10,... | collective-permute-start | bytes 258056 | tf_op jit(solution)/shard_map/ppermute | solution.py:428
  25.0 0.0 collective-permute-done.9
  25.0 0.5 %collective-permute-start.10 = (f32[144,128]{1,0:T(8,128)S(1)}, f32[144,128]{1,0:T(8,128)S(1)}, u32[]{:S(2)}, u32[]{:S(2)}) collective-permute-start(f32[144,128]{1,0:T(8,128)S(1)} %add.44), channel_id=1, source_target_pairs={{0,3},{1,4},{2,7},{3,0},{4,1},{5,6},{6,5},{7,2},{8,13},{9,10},{10,... | collective-permute-start | bytes 221192 | tf_op jit(solution)/shard_map/ppermute | solution.py:428
  25.6 2.4 %collective-permute-done.6 = f32[168,128]{1,0:T(8,128)S(1)} collective-permute-done((f32[168,128]{1,0:T(8,128)S(1)}, f32[168,128]{1,0:T(8,128)S(1)}, u32[]{:S(2)}, u32[]{:S(2)}) %collective-permute-start.6) | collective-permute-done | bytes 86048 | tf_op jit(solution)/shard_map/ppermute | solution.py:428
  28.0 2.5 %collective-permute-start.7 = (f32[168,128]{1,0:T(8,128)S(1)}, f32[168,128]{1,0:T(8,128)S(1)}, u32[]{:S(2)}, u32[]{:S(2)}) collective-permute-start(f32[168,128]{1,0:T(8,128)S(1)} %add.41), channel_id=1, source_target_pairs={{0,5},{1,8},{2,11},{3,6},{4,13},{5,0},{6,3},{7,14},{8,1},{9,12},{1... | collective-permute-start | bytes 258056 | tf_op jit(solution)/shard_map/ppermute | solution.py:428
  30.5 0.0 collective-permute-done.10
  30.5 0.8 %collective-permute-start.11 = (f32[144,128]{1,0:T(8,128)S(1)}, f32[144,128]{1,0:T(8,128)S(1)}, u32[]{:S(2)}, u32[]{:S(2)}) collective-permute-start(f32[144,128]{1,0:T(8,128)S(1)} %add.45), channel_id=1, source_target_pairs={{0,5},{1,8},{2,11},{3,6},{4,13},{5,0},{6,3},{7,14},{8,1},{9,12},{1... | collective-permute-start | bytes 221192 | tf_op jit(solution)/shard_map/ppermute | solution.py:428
  31.3 2.3 %collective-permute-done.7 = f32[168,128]{1,0:T(8,128)S(1)} collective-permute-done((f32[168,128]{1,0:T(8,128)S(1)}, f32[168,128]{1,0:T(8,128)S(1)}, u32[]{:S(2)}, u32[]{:S(2)}) %collective-permute-start.7) | collective-permute-done | bytes 86048 | tf_op jit(solution)/shard_map/ppermute | solution.py:428
  33.6 0.1 collective-permute-start.8
  33.7 1.6 %collective-permute-done.11 = f32[144,128]{1,0:T(8,128)S(1)} collective-permute-done((f32[144,128]{1,0:T(8,128)S(1)}, f32[144,128]{1,0:T(8,128)S(1)}, u32[]{:S(2)}, u32[]{:S(2)}) %collective-permute-start.11) | collective-permute-done | bytes 73760 | tf_op jit(solution)/shard_map/ppermute | solution.py:428
  35.3 0.4 collective-permute-start.12
  35.7 2.2 %collective-permute-done.8 = f32[168,128]{1,0:T(8,128)S(1)} collective-permute-done((f32[168,128]{1,0:T(8,128)S(1)}, f32[168,128]{1,0:T(8,128)S(1)}, u32[]{:S(2)}, u32[]{:S(2)}) %collective-permute-start.8) | collective-permute-done | bytes 86048 | tf_op jit(solution)/shard_map/ppermute | solution.py:428
  37.9 1.4 %collective-permute-start.13 = (f32[168,128]{1,0:T(8,128)S(1)}, f32[168,128]{1,0:T(8,128)S(1)}, u32[]{:S(2)}, u32[]{:S(2)}) collective-permute-start(f32[168,128]{1,0:T(8,128)S(1)} %add.43.refs_0_), channel_id=1, source_target_pairs={{0,1},{1,0},{2,3},{3,2},{4,5},{5,4},{6,7},{7,6},{8,9},{9,8},{10,11... | collective-permute-start | bytes 258056 | tf_op jit(solution)/shard_map/ppermute | solution.py:428
  39.3 0.0 collective-permute-done.12
  39.3 1.9 %collective-permute-start.14 = (f32[144,128]{1,0:T(8,128)S(1)}, f32[144,128]{1,0:T(8,128)S(1)}, u32[]{:S(2)}, u32[]{:S(2)}) collective-permute-start(f32[144,128]{1,0:T(8,128)S(1)} %add.47.refs_1_), channel_id=1, source_target_pairs={{0,1},{1,0},{2,3},{3,2},{4,5},{5,4},{6,7},{7,6},{8,9},{9,8},{10,11... | collective-permute-start | bytes 221192 | tf_op jit(solution)/shard_map/ppermute | solution.py:428
  41.3 0.9 %collective-permute-done.14.refs_3_ = f32[144,128]{1,0:T(8,128)S(1)} collective-permute-done((f32[144,128]{1,0:T(8,128)S(1)}, f32[144,128]{1,0:T(8,128)S(1)}, u32[]{:S(2)}, u32[]{:S(2)}) %collective-permute-start.14) | collective-permute-done | bytes 73760 | tf_op jit(solution)/shard_map/ppermute | solution.py:428
  42.2 0.0 collective-permute-done.13.refs_2_
  42.2 0.0 copy-done
  42.2 3.2 %shard_map.85 = f32[12,49,23,128]{3,2,1,0:T(8,128)} custom-call(s32[12]{0:T(128)S(1)} %copy-done.2, f32[12,52,23,128]{3,2,1,0:T(8,128)S(1)} %get-tuple-element.15.cells_ref, f32[12,32,128]{2,1,0:T(8,128)S(1)} %get-tuple-element.20.factor_ref.scaled_factor_ref, f32[736,128]{1,0:T(8,128)S(1)} %get-tuple-element.17.cross_factor_ref, f32[24,3136]{1,0:T(8,128)S(1)} %copy-done, ...), custom_call_target="tpu_custom_call" | custom-call | tf_op jit(solution)/shard_map/pallas_call | solution.py:400
  (12 shorter events, 0.1 us)
Async XLA Ops:
  0.0 21.4 %copy-start.2 = (s32[12]{0:T(128)S(1)}, s32[12]{0:T(128)}, u32[]{:S(2)}) copy-start(s32[12]{0:T(128)} %ids_ref.5) | copy-start | bytes 148
  0.0 21.4 %copy-start.1 = (f32[24,1472]{1,0:T(8,128)S(1)}, f32[24,1472]{1,0:T(8,128)}, u32[]{:S(2)}) copy-start(f32[24,1472]{1,0:T(8,128)} %target_ref.2) | copy-start | bytes 423940
  5.4 1.7 %collective-permute-start = (f32[144,128]{1,0:T(8,128)S(1)}, f32[144,128]{1,0:T(8,128)S(1)}, u32[]{:S(2)}, u32[]{:S(2)}) collective-permute-start(f32[144,128]{1,0:T(8,128)S(1)} %get-tuple-element.19), channel_id=1, source_target_pairs={{0,1},{1,0},{2,3},{3,2},{4,5},{5,4},{6,7},{7,6},{8,9},{9,8},{10,11... | collective-permute-start | bytes 221192 | tf_op jit(solution)/shard_map/ppermute | solution.py:428
  7.1 3.8 %collective-permute-start.1 = (f32[144,128]{1,0:T(8,128)S(1)}, f32[144,128]{1,0:T(8,128)S(1)}, u32[]{:S(2)}, u32[]{:S(2)}) collective-permute-start(f32[144,128]{1,0:T(8,128)S(1)} %add.36), channel_id=1, source_target_pairs={{0,3},{1,4},{2,7},{3,0},{4,1},{5,6},{6,5},{7,2},{8,13},{9,10},{10,... | collective-permute-start | bytes 221192 | tf_op jit(solution)/shard_map/ppermute | solution.py:428
  10.9 5.3 %collective-permute-start.2 = (f32[144,128]{1,0:T(8,128)S(1)}, f32[144,128]{1,0:T(8,128)S(1)}, u32[]{:S(2)}, u32[]{:S(2)}) collective-permute-start(f32[144,128]{1,0:T(8,128)S(1)} %add.37), channel_id=1, source_target_pairs={{0,5},{1,8},{2,11},{3,6},{4,13},{5,0},{6,3},{7,14},{8,1},{9,12},{1... | collective-permute-start | bytes 221192 | tf_op jit(solution)/shard_map/ppermute | solution.py:428
  16.2 3.8 %collective-permute-start.3 = (f32[144,128]{1,0:T(8,128)S(1)}, f32[144,128]{1,0:T(8,128)S(1)}, u32[]{:S(2)}, u32[]{:S(2)}) collective-permute-start(f32[144,128]{1,0:T(8,128)S(1)} %add.38), channel_id=1, source_target_pairs={{0,9},{1,2},{2,1},{3,10},{4,7},{5,12},{6,15},{7,4},{8,11},{9,0},{1... | collective-permute-start | bytes 221192 | tf_op jit(solution)/shard_map/ppermute | solution.py:428
  20.1 1.3 %collective-permute-start.4 = (f32[144,128]{1,0:T(8,128)S(1)}, f32[144,128]{1,0:T(8,128)S(1)}, u32[]{:S(2)}, u32[]{:S(2)}) collective-permute-start(f32[144,128]{1,0:T(8,128)S(1)} %add.39.own_ref), channel_id=1, source_target_pairs={{0,1},{1,0},{2,3},{3,2},{4,5},{5,4},{6,7},{7,6},{8,9},{9,8},{10,11... | collective-permute-start | bytes 221192 | tf_op jit(solution)/shard_map/ppermute | solution.py:428
  21.4 20.8 %copy-start = (f32[24,3136]{1,0:T(8,128)S(1)}, f32[24,3136]{1,0:T(8,128)}, u32[]{:S(2)}) copy-start(f32[24,3136]{1,0:T(8,128)} %target_ref.3) | copy-start | bytes 903172
  22.3 1.3 %collective-permute-start.5 = (f32[168,128]{1,0:T(8,128)S(1)}, f32[168,128]{1,0:T(8,128)S(1)}, u32[]{:S(2)}, u32[]{:S(2)}) collective-permute-start(f32[168,128]{1,0:T(8,128)S(1)} %get-tuple-element.22), channel_id=1, source_target_pairs={{0,1},{1,0},{2,3},{3,2},{4,5},{5,4},{6,7},{7,6},{8,9},{9,8},{10,11... | collective-permute-start | bytes 258056 | tf_op jit(solution)/shard_map/ppermute | solution.py:428
  22.6 2.4 %collective-permute-start.9 = (f32[144,128]{1,0:T(8,128)S(1)}, f32[144,128]{1,0:T(8,128)S(1)}, u32[]{:S(2)}, u32[]{:S(2)}) collective-permute-start(f32[144,128]{1,0:T(8,128)S(1)} %get-tuple-element.24), channel_id=1, source_target_pairs={{0,1},{1,0},{2,3},{3,2},{4,5},{5,4},{6,7},{7,6},{8,9},{9,8},{10,11... | collective-permute-start | bytes 221192 | tf_op jit(solution)/shard_map/ppermute | solution.py:428
  23.7 4.3 %collective-permute-start.6 = (f32[168,128]{1,0:T(8,128)S(1)}, f32[168,128]{1,0:T(8,128)S(1)}, u32[]{:S(2)}, u32[]{:S(2)}) collective-permute-start(f32[168,128]{1,0:T(8,128)S(1)} %add.40), channel_id=1, source_target_pairs={{0,3},{1,4},{2,7},{3,0},{4,1},{5,6},{6,5},{7,2},{8,13},{9,10},{10,... | collective-permute-start | bytes 258056 | tf_op jit(solution)/shard_map/ppermute | solution.py:428
  25.0 5.5 %collective-permute-start.10 = (f32[144,128]{1,0:T(8,128)S(1)}, f32[144,128]{1,0:T(8,128)S(1)}, u32[]{:S(2)}, u32[]{:S(2)}) collective-permute-start(f32[144,128]{1,0:T(8,128)S(1)} %add.44), channel_id=1, source_target_pairs={{0,3},{1,4},{2,7},{3,0},{4,1},{5,6},{6,5},{7,2},{8,13},{9,10},{10,... | collective-permute-start | bytes 221192 | tf_op jit(solution)/shard_map/ppermute | solution.py:428
  28.0 5.6 %collective-permute-start.7 = (f32[168,128]{1,0:T(8,128)S(1)}, f32[168,128]{1,0:T(8,128)S(1)}, u32[]{:S(2)}, u32[]{:S(2)}) collective-permute-start(f32[168,128]{1,0:T(8,128)S(1)} %add.41), channel_id=1, source_target_pairs={{0,5},{1,8},{2,11},{3,6},{4,13},{5,0},{6,3},{7,14},{8,1},{9,12},{1... | collective-permute-start | bytes 258056 | tf_op jit(solution)/shard_map/ppermute | solution.py:428
  30.5 4.7 %collective-permute-start.11 = (f32[144,128]{1,0:T(8,128)S(1)}, f32[144,128]{1,0:T(8,128)S(1)}, u32[]{:S(2)}, u32[]{:S(2)}) collective-permute-start(f32[144,128]{1,0:T(8,128)S(1)} %add.45), channel_id=1, source_target_pairs={{0,5},{1,8},{2,11},{3,6},{4,13},{5,0},{6,3},{7,14},{8,1},{9,12},{1... | collective-permute-start | bytes 221192 | tf_op jit(solution)/shard_map/ppermute | solution.py:428
  33.6 4.3 %collective-permute-start.8 = (f32[168,128]{1,0:T(8,128)S(1)}, f32[168,128]{1,0:T(8,128)S(1)}, u32[]{:S(2)}, u32[]{:S(2)}) collective-permute-start(f32[168,128]{1,0:T(8,128)S(1)} %add.42), channel_id=1, source_target_pairs={{0,9},{1,2},{2,1},{3,10},{4,7},{5,12},{6,15},{7,4},{8,11},{9,0},{1... | collective-permute-start | bytes 258056 | tf_op jit(solution)/shard_map/ppermute | solution.py:428
  35.3 4.0 %collective-permute-start.12 = (f32[144,128]{1,0:T(8,128)S(1)}, f32[144,128]{1,0:T(8,128)S(1)}, u32[]{:S(2)}, u32[]{:S(2)}) collective-permute-start(f32[144,128]{1,0:T(8,128)S(1)} %add.46), channel_id=1, source_target_pairs={{0,9},{1,2},{2,1},{3,10},{4,7},{5,12},{6,15},{7,4},{8,11},{9,0},{1... | collective-permute-start | bytes 221192 | tf_op jit(solution)/shard_map/ppermute | solution.py:428
  37.9 4.3 %collective-permute-start.13 = (f32[168,128]{1,0:T(8,128)S(1)}, f32[168,128]{1,0:T(8,128)S(1)}, u32[]{:S(2)}, u32[]{:S(2)}) collective-permute-start(f32[168,128]{1,0:T(8,128)S(1)} %add.43.refs_0_), channel_id=1, source_target_pairs={{0,1},{1,0},{2,3},{3,2},{4,5},{5,4},{6,7},{7,6},{8,9},{9,8},{10,11... | collective-permute-start | bytes 258056 | tf_op jit(solution)/shard_map/ppermute | solution.py:428
  39.3 2.9 %collective-permute-start.14 = (f32[144,128]{1,0:T(8,128)S(1)}, f32[144,128]{1,0:T(8,128)S(1)}, u32[]{:S(2)}, u32[]{:S(2)}) collective-permute-start(f32[144,128]{1,0:T(8,128)S(1)} %add.47.refs_1_), channel_id=1, source_target_pairs={{0,1},{1,0},{2,3},{3,2},{4,5},{5,4},{6,7},{7,6},{8,9},{9,8},{10,11... | collective-permute-start | bytes 221192 | tf_op jit(solution)/shard_map/ppermute | solution.py:428
